TPU v7x, 32 devices: a whole 2x2x4 slice. The times are simulated.
32 devices in a mesh: groups: 2 (over y), dp: 4 (over z), tensor: 4 (over x, core).
Axes of the slice: x: 2, y: 2, z: 4, core: 2. Of those that a mesh axis runs over, the one named last changes fastest.
Arguments:
- queries: bfloat16 [96, 128, 576], P(('groups', 'dp'), 'tensor'), parts along dimension 0, may hold values from -4 to 4
- latent_cache: bfloat16 [96, 128, 576], P(('groups', 'dp')), parts along dimension 0, may hold values from -4 to 4
- lengths: int32 [96], P(('groups', 'dp')), parts along dimension 0, may hold values from 2 to 128, as said below
- value_up: bfloat16 [128, 512, 128], P('tensor'), may hold values from -0.25 to 0.25
- out_proj: bfloat16 [16384, 7168], P('tensor', 'dp'), may hold values from -0.046875 to 0.046875
- residual: bfloat16 [96, 7168], P('groups', 'dp'), parts along dimension 0, may hold values from -1.5 to 1.5
- expert_ids: int32 [96, 8], P('groups'), parts along dimension 0, may hold values from 0 to 255, as said below
- gate_weights: float32 [96, 8], P('groups'), parts along dimension 0, may hold values from 0.1 to 1
- placement: int32 [512], P('groups'), parts along dimension 0, may hold values from 0 to 255, as said below
- norm_gain: bfloat16 [7168], replicated, may hold values from 0.5 to 1.5
- w_gate: bfloat16 [4, 7168, 2048], P('dp', None, 'tensor'), may hold values from -0.0625 to 0.0625
- w_up: bfloat16 [4, 7168, 2048], P('dp', None, 'tensor'), may hold values from -0.0625 to 0.0625
Outputs:
- attn_out: bfloat16 [96, 7168], P('groups', ('dp', 'tensor')), parts along dimension 0
- expert_hidden: bfloat16 [8, 3, 2048], P(('groups', 'dp'), None, 'tensor'), parts along dimension 0
There are 2 independent parts, one for each index of `groups`. A program takes and returns all parts, laid end to end along the dimension named above; an argument that names none is the same for every part. Nothing has to cross between parts.
Inputs may be any that keep to these rules, and one draw needn't show every extreme that they name: `lengths`: in every draw some request has all 128 positions cached. `expert_ids`: each row names 8 different experts. `placement`: a permutation of 0 to 255; in every draw some expert at a position under 4 is named by 3 rows or more.
All inputs are finite; a program needn't handle non-finite values.
Results may differ from a plain program's by a relative error of at most 0.0088.
Values may be sent and summed in bfloat16 or wider, within the bound.
A program may use at most 128 MiB of HBM per device.

v0:
```python
import jax
import jax.numpy as jnp
from jax import lax
from jax.sharding import PartitionSpec as P

LATENT = 512
ROPE = 64
VHEAD = 128
EXPERTS = 256
TOPK = 8


def slot_table(expert_ids, placement, held_count, capacity):
    flat_ids = expert_ids.reshape(-1)
    id_match = flat_ids[:, None] == jnp.arange(EXPERTS, dtype=jnp.int32)[None, :]
    position = jnp.sum(jnp.where(id_match, placement[None, :], 0), axis=1)
    chosen = (position[:, None] == jnp.arange(held_count, dtype=jnp.int32)[None, :]).astype(
        jnp.int32
    )
    earlier = jnp.cumsum(chosen, axis=0) - chosen
    slot_index = jnp.sum(chosen * earlier, axis=1)
    kept_slot = (position < held_count) & (slot_index < capacity)
    target = jnp.where(kept_slot, position * capacity + slot_index, held_count * capacity)
    return target.reshape(expert_ids.shape)


def on_device(
    queries,
    latent_cache,
    lengths,
    value_up,
    out_proj,
    residual,
    expert_ids,
    gate_weights,
    placement,
    norm_gain,
    w_gate,
    w_up,
):
    dp_count = lax.axis_size("dp")
    tensor_count = lax.axis_size("tensor")
    token_count = expert_ids.shape[0]
    local_experts = w_gate.shape[0]
    held_count = local_experts * dp_count
    capacity = max(2, token_count * TOPK * 2 // EXPERTS)
    score_scale = (VHEAD + ROPE) ** (-0.5)
    scores = (
        jnp.einsum("thc,tsc->ths", queries, latent_cache, preferred_element_type=jnp.float32)
        * score_scale
    )
    live_keys = (
        jnp.arange(latent_cache.shape[1], dtype=jnp.int32)[None, None, :] < lengths[:, None, None]
    )
    scores = jnp.where(live_keys, scores, -jnp.inf)
    row_max = jnp.max(scores, axis=2, keepdims=True)
    exponent = jnp.exp(scores - row_max)
    attention_weights = (exponent / jnp.sum(exponent, axis=2, keepdims=True)).astype(jnp.bfloat16)
    context = jnp.einsum(
        "ths,tsc->thc",
        attention_weights,
        latent_cache[:, :, :LATENT],
        preferred_element_type=jnp.float32,
    ).astype(jnp.bfloat16)
    head_out = jnp.einsum(
        "thc,hcv->thv", context, value_up, preferred_element_type=jnp.float32
    ).astype(jnp.bfloat16)
    head_out = head_out.reshape(head_out.shape[0], -1)
    partial_sum = jnp.dot(
        lax.all_gather(head_out, "dp", axis=0, tiled=True),
        out_proj,
        preferred_element_type=jnp.float32,
    )
    target = slot_table(expert_ids, placement, held_count, capacity)
    slot_ids = jnp.arange(held_count * capacity, dtype=jnp.int32)
    slot_match = target[:, :, None] == slot_ids[None, None, :]
    onehot = jnp.any(slot_match, axis=1).astype(jnp.bfloat16)
    gate_all = jnp.sum(jnp.where(slot_match, gate_weights[:, :, None], 0.0), axis=(0, 1))
    owner_span = local_experts * capacity
    owner_index = lax.axis_index("dp")
    slot_gate = lax.dynamic_slice_in_dim(gate_all, owner_index * owner_span, owner_span).reshape(
        local_experts, capacity
    )
    gain_values = norm_gain.astype(jnp.float32)
    tensor_pos = lax.axis_index("tensor")
    summed_all = lax.psum(partial_sum, "tensor")
    stream_cols = (summed_all + residual.astype(jnp.float32)).astype(jnp.bfloat16)
    col_width = stream_cols.shape[1] // tensor_count
    attn_out = lax.dynamic_slice_in_dim(stream_cols, tensor_pos * col_width, col_width, 1)
    buffer = jnp.einsum(
        "td,tc->dc", onehot, stream_cols, preferred_element_type=jnp.float32
    ).astype(jnp.bfloat16)
    buffer = buffer.reshape(held_count, capacity, -1)
    values = lax.all_to_all(buffer, "dp", split_axis=0, concat_axis=2, tiled=True).astype(
        jnp.float32
    )
    mean_square = jnp.mean(values * values, axis=-1, keepdims=True)
    normed = (values * lax.rsqrt(mean_square + 1e-06) * gain_values).astype(jnp.bfloat16)
    gate_proj = jnp.einsum("end,edf->enf", normed, w_gate, preferred_element_type=jnp.float32)
    up_proj = jnp.einsum("end,edf->enf", normed, w_up, preferred_element_type=jnp.float32)
    hidden = jax.nn.silu(gate_proj) * up_proj
    result = (slot_gate[:, :, None] * hidden).astype(jnp.bfloat16)
    return (attn_out, result)


def solution(mesh):
    in_specs = (
        P(("groups", "dp"), "tensor", None),
        P(("groups", "dp"), None, None),
        P(("groups", "dp")),
        P("tensor", None, None),
        P("tensor", "dp"),
        P("groups", "dp"),
        P("groups", None),
        P("groups", None),
        P("groups"),
        P(),
        P("dp", None, "tensor"),
        P("dp", None, "tensor"),
    )
    out_specs = (P("groups", ("dp", "tensor")), P(("groups", "dp"), None, "tensor"))
    return jax.shard_map(
        on_device, mesh=mesh, in_specs=in_specs, out_specs=out_specs, check_vma=False
    )
```

profile of v0, /device:TPU:0, one launch (start us, length us, event | category | flops | bytes accessed | tf_op | source)
XLA Modules:
  0.0 103.8 jit_solution(11480975397589859043)
XLA Ops:
  7.2 0.8 iota_compare_fusion.3
  8.0 0.2 copy-done
  8.2 1.9 %fusion.11 = f32[12,32,128]{2,1,0:T(8,128)S(1)} fusion(bf16[12,32,576]{2,1,0:T(8,128)(2,1)S(1)} %copy-done, bf16[12,128,576]{1,2,0:T(8,128)(2,1)} %param.13, pred[12,128]{1,0:T(8,128)(4,1)S(1)} %iota_compare_fusion.3), kind=kOutput, calls=%fused_computation.12 | convolution fusion | flops 56721408 | bytes 2409984 | tf_op jit(solution)/shard_map/thc,tsc->ths/dot_general | solution.py:49
  10.1 0.2 fusion.37
  10.3 2.1 %fusion.7 = bf16[12,32,512]{2,1,0:T(8,128)(2,1)S(1)} fusion(bf16[12,128,576]{1,2,0:T(8,128)(2,1)} %param.13, f32[12,32]{1,0:T(8,128)S(1)} %fusion.37, f32[12,32,128]{2,1,0:T(8,128)S(1)} %fusion.11), kind=kOutput, calls=%fused_computation.8 | convolution fusion | flops 50676224 | bytes 2367488 | tf_op jit(solution)/shard_map/ths,tsc->thc/dot_general | solution.py:59
  12.4 3.0 %fusion.13 = bf16[12,32,128]{2,0,1:T(8,128)(2,1)S(1)} fusion(bf16[32,512,128]{2,1,0:T(8,128)(2,1)} %param.15, bf16[12,32,512]{2,1,0:T(8,128)(2,1)S(1)} %fusion.7), kind=kOutput, calls=%fused_computation.14 | convolution fusion | flops 50380800 | bytes 4685824 | tf_op jit(solution)/shard_map/thc,hcv->thv/dot_general | solution.py:65
  15.5 17.4 %all-gather = bf16[4,12,4096]{2,1,0:T(8,128)(2,1)S(1)} all-gather(bf16[1,12,4096]{2,1,0:T(8,128)(2,1)S(1)} %reshape.186), channel_id=1, replica_groups=mesh['groups'=2,'dp'=4,'tensor'=4] {'dp'}, dimensions={0}, use_global_device_ids=true | all-gather | bytes 491520 | tf_op jit(solution)/shard_map/all_gather | solution.py:70
  33.1 8.5 %fusion.38 = f32[48,1792]{1,0:T(8,128)} fusion(bf16[48,4096]{1,0:T(8,128)(2,1)S(1)} %reshape.187, bf16[4096,1792]{1,0:T(8,128)(2,1)} %param.16), kind=kOutput, calls=%fused_computation.49 | convolution fusion | flops 704643072 | bytes 15417344 | tf_op jit(solution)/shard_map/dot_general | solution.py:69
  41.8 0.2 select_reduce_fusion
  42.0 1.2 %reduce-window.6 = s32[4,3,128]{2,1,0:T(4,128)S(1)} reduce-window(s32[4,3,128]{2,1,0:T(4,128)S(1)} %fusion.32, s32[]{:T(128)} %constant.9.clone.1), window={size=1x1x128 pad=0_0x0_0x127_0}, to_apply=%region_4.5 | reduce-window | flops 195072 | bytes 12292 | tf_op jit(solution)/shard_map/reduce-window
  43.3 0.2 slice_reduce_fusion
  43.5 0.2 reduce-window.9
  44.0 0.2 select_reduce_fusion.1
  44.3 31.4 %all-reduce.2.cloned.1.call-done = f32[48,1792]{1,0:T(8,128)} async-done(((f32[48,1792]{1,0:T(8,128)}), f32[48,1792]{1,0:T(8,128)}) %all-reduce.2.cloned.1.call-update) | async-done | bytes 344080 | tf_op jit(solution)/shard_map/psum | solution.py:86
  75.7 1.0 add_convert_fusion
  76.7 0.1 convolution_convert_fusion
  76.8 0.7 reshape.181
  77.5 4.6 %all-to-all-start = ((bf16[4,3,1792]{2,1,0:T(4,128)(2,1)}), bf16[4,3,1792]{2,1,0:T(4,128)(2,1)S(1)}, u32[]{:S(2)}, u32[]{:S(2)}) async-start(bf16[4,3,1792]{2,1,0:T(4,128)(2,1)} %reshape.181), calls=%async_computation | async-start | bytes 114688 | tf_op jit(solution)/shard_map/all_to_all | solution.py:94
  82.1 0.7 constant_dynamic-slice_fusion
  82.8 5.0 %all-to-all-done = bf16[4,3,1792]{2,1,0:T(4,128)(2,1)S(1)} async-done(((bf16[4,3,1792]{2,1,0:T(4,128)(2,1)}), bf16[4,3,1792]{2,1,0:T(4,128)(2,1)S(1)}, u32[]{:S(2)}, u32[]{:S(2)}) %all-to-all-start) | async-done | bytes 43040 | tf_op jit(solution)/shard_map/all_to_all | solution.py:94
  87.8 0.2 fusion.27
  88.0 0.1 fusion.29
  88.1 4.1 %fusion.3 = f32[3,512]{1,0:T(4,128)S(1)} fusion(bf16[3,7168]{1,0:T(4,128)(2,1)S(1)} %bitcast.56, bf16[1,7168,512]{2,1,0:T(8,128)(2,1)} %param.22), kind=kOutput, calls=%fused_computation.3 | convolution fusion | flops 22020096 | bytes 7389184 | tf_op jit(solution)/shard_map/end,edf->enf/dot_general | solution.py:99
  92.2 4.8 %fusion.23 = bf16[1,3,512]{2,1,0:T(4,128)(2,1)} fusion(bf16[3,7168]{1,0:T(4,128)(2,1)S(1)} %bitcast.57, bf16[1,7168,512]{2,1,0:T(8,128)(2,1)} %param.23, f32[3,512]{1,0:T(4,128)S(1)} %fusion.3, f32[3]{0:T(128)S(1)} %dynamic_slice.7), kind=kOutput, calls=%fused_computation.18 | convolution fusion | flops 22030848 | bytes 7392268 | tf_op jit(solution)/shard_map/end,edf->enf/dot_general | solution.py:100
  (28 shorter events, 0.9 us)
Async XLA Ops:
  7.2 1.1 %copy-start = (bf16[12,32,576]{2,1,0:T(8,128)(2,1)S(1)}, bf16[12,32,576]{2,1,0:T(8,128)(2,1)}, u32[]{:S(2)}) copy-start(bf16[12,32,576]{2,1,0:T(8,128)(2,1)} %param.12) | copy-start | bytes 1327108
  7.2 68.5 %all-reduce.2.cloned.1.call-start = ((), (), s32[]{:S(2)}) async-start(), calls=%async_computation.1 | async-start | bytes 688128 | tf_op jit(solution)/shard_map/psum | solution.py:86
  33.0 8.6 %copy-start.3 = (s32[48,8]{0,1:T(8,128)S(1)}, s32[48,8]{0,1:T(8,128)}, u32[]{:S(2)}) copy-start(s32[48,8]{0,1:T(8,128)} %param.18) | copy-start | bytes 4612
  33.0 8.8 %copy-start.5 = (s32[256]{0:T(256)S(1)}, s32[256]{0:T(256)}, u32[]{:S(2)}) copy-start(s32[256]{0:T(256)} %param.20) | copy-start | bytes 3076
  33.0 10.9 %copy-start.2 = (bf16[7168]{0:T(1024)(128)(2,1)S(1)}, bf16[7168]{0:T(1024)(128)(2,1)}, u32[]{:S(2)}) copy-start(bf16[7168]{0:T(1024)(128)(2,1)} %param.21) | copy-start | bytes 43012
  33.0 10.9 %copy-start.4 = (f32[48,8]{0,1:T(8,128)S(1)}, f32[48,8]{0,1:T(8,128)}, u32[]{:S(2)}) copy-start(f32[48,8]{0,1:T(8,128)} %param.19) | copy-start | bytes 4612
  33.1 42.6 %copy-start.1 = (bf16[48,1792]{1,0:T(8,128)(2,1)S(1)}, bf16[48,1792]{1,0:T(8,128)(2,1)}, u32[]{:S(2)}) copy-start(bf16[48,1792]{1,0:T(8,128)(2,1)} %param.17) | copy-start | bytes 516100
  77.5 10.3 %all-to-all-start = ((bf16[4,3,1792]{2,1,0:T(4,128)(2,1)}), bf16[4,3,1792]{2,1,0:T(4,128)(2,1)S(1)}, u32[]{:S(2)}, u32[]{:S(2)}) async-start(bf16[4,3,1792]{2,1,0:T(4,128)(2,1)} %reshape.181), calls=%async_computation | async-start | bytes 114688 | tf_op jit(solution)/shard_map/all_to_all | solution.py:94
Sparse Core Ops, SparseCore 0:
  41.7 33.8 all-reduce.1
where the time goes:
time: 104 us
  waiting for transfers between devices  36.4 us (35%)
  matrix products  24.5 us (24%)
  blocking collectives  17.4 us (17%)
  between operations  14.2 us (14%)
  starting transfers between devices  4.64 us (4%)
  other arithmetic  4.23 us (4%)
  local copies, waits for them, and re-layouts  2.47 us (2%)
    psum x1, waiting for transfers between devices, on_device(): summed_all = lax.psum(partial_sum, 'tensor')  31.4 us
    all_gather x1, blocking collectives, on_device(): lax.all_gather(head_out, 'dp', axis=0, tiled=True)  17.4 us
    dot_general x1, matrix products, on_device(): jnp.dot(lax.all_gather(head_out, 'dp', axis=0, tiled=True), out_proj, pre...  8.53 us
    all_to_all x1, waiting for transfers between devices, on_device(): lax.all_to_all(buffer, 'dp', split_axis=0, concat_axis=2, tiled=True)  5.02 us
    dot_general x1, matrix products, on_device(): jnp.einsum('end,edf->enf', normed, w_up, preferred_element_type=jnp.float32)  4.75 us
    all_to_all x1, starting transfers between devices, on_device(): lax.all_to_all(buffer, 'dp', split_axis=0, concat_axis=2, tiled=True)  4.6 us
    dot_general x1, matrix products, on_device(): jnp.einsum('end,edf->enf', normed, w_gate, preferred_element_type=jnp.flo...  4.13 us
    dot_general x1, matrix products, on_device(): jnp.einsum('thc,hcv->thv', context, value_up, preferred_element_type=jnp....  2.97 us
  transfers between devices with their start and end apart: 2, of which 2 were waited for; matrix products, arithmetic and copies ran while one was open for 3% of the time, Pallas kernels for 0%

commit v1 on v0

--- a/solution.py
+++ b/solution.py
@@ -1,6 +1,10 @@
+import functools
+
 import jax
 import jax.numpy as jnp
 from jax import lax
+from jax.experimental import pallas as pl
+from jax.experimental.pallas import tpu as pltpu
 from jax.sharding import PartitionSpec as P
 
 LATENT = 512
@@ -8,6 +12,460 @@
 VHEAD = 128
 EXPERTS = 256
 TOPK = 8
+F32 = jnp.float32
+BF16 = jnp.bfloat16
+MESH = pl.DeviceIdType.MESH
+
+
+def layer_kernel(
+    dp_count,
+    tp_count,
+    q_hbm,
+    cache_hbm,
+    len_ref,
+    vu_hbm,
+    wo_hbm,
+    res_ref,
+    ids_ref,
+    gates_ref,
+    place_ref,
+    gain_ref,
+    wg_hbm,
+    wu_hbm,
+    attn_ref,
+    hid_ref,
+    q_s,
+    cache_s,
+    vu_s,
+    wo_s,
+    wg_s,
+    wu_s,
+    ctx_s,
+    hbuf,
+    acc_s,
+    stg,
+    own_s,
+    red_send,
+    red_recv,
+    onehot_s,
+    disp,
+    xrecv,
+    sg_s,
+    in_sem,
+    vu_sem,
+    wo_sem,
+    we_sem,
+    ag_send,
+    ag_recv,
+    rs_send,
+    rs_recv,
+    dx_send,
+    dx_recv,
+):
+    g = lax.axis_index("groups")
+    d = lax.axis_index("dp")
+    t = lax.axis_index("tensor")
+    peers = dp_count * tp_count
+    me = d * tp_count + t
+    tokens, heads, width = q_s.shape
+    rows_pad = ctx_s.shape[1] // heads
+    chunks = hbuf.shape[0]
+    hpc = heads // chunks
+    kc = hpc * VHEAD
+    cols = attn_ref.shape[1]
+    pad = own_s.shape[2]
+    all_tokens = attn_ref.shape[0]
+    model = wg_hbm.shape[1]
+    ff = wg_hbm.shape[2]
+    capacity = hid_ref.shape[1]
+
+    q_copy = pltpu.make_async_copy(q_hbm, q_s, in_sem.at[0])
+    c_copy = pltpu.make_async_copy(cache_hbm, cache_s, in_sem.at[1])
+    q_copy.start()
+    c_copy.start()
+
+    barrier = pltpu.get_barrier_semaphore()
+    for o in range(1, peers):
+        other = lax.rem(me + o, peers)
+        pl.semaphore_signal(
+            barrier,
+            inc=1,
+            device_id=(g, other // tp_count, lax.rem(other, tp_count)),
+            device_id_type=MESH,
+        )
+
+    vu_copies = [
+        pltpu.make_async_copy(
+            vu_hbm.at[pl.ds(c * hpc, hpc)], vu_s.at[pl.ds(c * hpc, hpc)], vu_sem.at[c]
+        )
+        for c in range(chunks)
+    ]
+    wo_copies = [
+        pltpu.make_async_copy(
+            wo_hbm.at[pl.ds(c * kc, kc)], wo_s.at[pl.ds(c * kc, kc)], wo_sem.at[c]
+        )
+        for c in range(chunks)
+    ]
+    wg_copy = pltpu.make_async_copy(wg_hbm.at[0], wg_s.at[pl.ds(0, model)], we_sem.at[0])
+    wu_copy = pltpu.make_async_copy(wu_hbm.at[0], wu_s.at[pl.ds(0, model)], we_sem.at[1])
+    for cp in vu_copies:
+        cp.start()
+
+    ids = ids_ref[...]
+    gates = gates_ref[...]
+    place = place_ref[...]
+    expert_iota = lax.broadcasted_iota(jnp.int32, place.shape, 1)
+
+    def choice(position):
+        expert = jnp.sum(jnp.where(place == position, expert_iota, 0), axis=1, keepdims=True)
+        return ids == expert
+
+    row8 = lax.broadcasted_iota(jnp.int32, (8, all_tokens), 0)
+    match = jnp.zeros((8, all_tokens), F32)
+    for p in range(dp_count):
+        hit = jnp.sum(choice(p).astype(F32), axis=0, keepdims=True)
+        match = jnp.where(row8 == p, hit, match)
+    own_choice = choice(d)
+    own_hit = jnp.sum(own_choice.astype(F32), axis=0, keepdims=True)
+    own_gate = jnp.sum(jnp.where(own_choice, gates, 0.0), axis=0, keepdims=True)
+    match = jnp.where(row8 == dp_count, own_hit, match)
+    up_r = lax.broadcasted_iota(jnp.int32, (all_tokens, all_tokens), 0)
+    up_c = lax.broadcasted_iota(jnp.int32, (all_tokens, all_tokens), 1)
+    upper = jnp.where(up_r < up_c, 1.0, 0.0).astype(BF16)
+    earlier = jnp.dot(match.astype(BF16), upper, preferred_element_type=F32)
+    shape = (16 * dp_count, all_tokens)
+    rep_m = jnp.concatenate(
+        [jnp.broadcast_to(match[p : p + 1], (16, all_tokens)) for p in range(dp_count)], axis=0
+    )
+    rep_e = jnp.concatenate(
+        [jnp.broadcast_to(earlier[p : p + 1], (16, all_tokens)) for p in range(dp_count)], axis=0
+    )
+    r_iota = lax.broadcasted_iota(jnp.int32, shape, 0)
+    slot = r_iota & 3
+    quarter = (r_iota >> 2) & 3
+    kept = jnp.where((rep_e == slot.astype(F32)) & (slot < capacity), rep_m, 0.0)
+    for q in range(4):
+        onehot_s[q] = jnp.where(quarter == q, kept, 0.0).astype(BF16)
+    own_e = jnp.broadcast_to(earlier[dp_count : dp_count + 1], (8, all_tokens))
+    own_g = jnp.broadcast_to(own_gate * own_hit, (8, all_tokens))
+    sg_s[...] = jnp.broadcast_to(
+        jnp.sum(
+            jnp.where((own_e == row8.astype(F32)) & (row8 < capacity), own_g, 0.0),
+            axis=1,
+            keepdims=True,
+        ),
+        sg_s.shape,
+    )
+
+    ctx_s[...] = jnp.zeros_like(ctx_s)
+    wg_s[pl.ds(model, wg_s.shape[0] - model), :] = jnp.zeros((wg_s.shape[0] - model, ff), BF16)
+    wu_s[pl.ds(model, wu_s.shape[0] - model), :] = jnp.zeros((wu_s.shape[0] - model, ff), BF16)
+    stg[:, pl.ds(tp_count * cols, stg.shape[1] - tp_count * cols)] = jnp.zeros(
+        (all_tokens, stg.shape[1] - tp_count * cols), F32
+    )
+
+    q_copy.wait()
+    c_copy.wait()
+    for cp in wo_copies:
+        cp.start()
+    wg_copy.start()
+    wu_copy.start()
+
+    score_scale = (VHEAD + ROPE) ** (-0.5)
+    ctx_len = cache_s.shape[2]
+
+    def token_step(i, carry):
+        scores = jnp.dot(q_s[i], cache_s[i], preferred_element_type=F32) * score_scale
+        live = lax.broadcasted_iota(jnp.int32, (heads, ctx_len), 1) < len_ref[i]
+        scores = jnp.where(live, scores, -jnp.inf)
+        top = jnp.max(scores, axis=1, keepdims=True)
+        e = jnp.exp(scores - top)
+        w = (e / jnp.sum(e, axis=1, keepdims=True)).astype(BF16)
+        context = lax.dot_general(
+            w,
+            cache_s[i, pl.ds(0, LATENT), :],
+            (((1,), (1,)), ((), ())),
+            preferred_element_type=F32,
+        )
+        for k in range(LATENT // 128):
+            ctx_s[k, pl.ds(i, heads, stride=rows_pad), :] = context[:, k * 128 : (k + 1) * 128]
+        return carry
+
+    lax.fori_loop(0, tokens, token_step, 0, unroll=UNROLL)
+
+    def ag_copy(c, o):
+        peer = lax.rem(d + o, dp_count)
+        return pltpu.make_async_remote_copy(
+            src_ref=hbuf.at[c, d],
+            dst_ref=hbuf.at[c, d],
+            send_sem=ag_send.at[c, o],
+            recv_sem=ag_recv.at[c, d],
+            device_id=(g, peer, t),
+            device_id_type=MESH,
+        )
+
+    def ag_arrival(c, o):
+        src = lax.rem(d + o, dp_count)
+        return pltpu.make_async_remote_copy(
+            src_ref=hbuf.at[c, src],
+            dst_ref=hbuf.at[c, src],
+            send_sem=ag_send.at[c, o],
+            recv_sem=ag_recv.at[c, src],
+            device_id=(g, src, t),
+            device_id_type=MESH,
+        )
+
+    for c in range(chunks):
+        vu_copies[c].wait()
+        for hl in range(hpc):
+            h = c * hpc + hl
+            rows = jnp.concatenate(
+                [ctx_s[k, pl.ds(h * rows_pad, rows_pad), :] for k in range(LATENT // 128)], axis=1
+            ).astype(BF16)
+            out = jnp.dot(rows, vu_s[h], preferred_element_type=F32)
+            hbuf[c, d, :, pl.ds(hl * VHEAD, VHEAD)] = out.astype(BF16)
+        if c == 0:
+            pl.semaphore_wait(barrier, peers - 1)
+        for o in range(1, dp_count):
+            ag_copy(c, o).start()
+
+    acc_s[...] = jnp.zeros_like(acc_s)
+    n_tile = 256
+    n_count = wo_s.shape[1] // n_tile
+    for c in range(chunks):
+        wo_copies[c].wait()
+        for o in range(1, dp_count):
+            ag_arrival(c, o).wait_recv()
+        left = hbuf[c].reshape(dp_count * rows_pad, kc)
+
+        def n_step(n, carry, c=c, left=left):
+            sl = pl.ds(pl.multiple_of(n * n_tile, n_tile), n_tile)
+            acc_s[:, sl] += jnp.dot(
+                left, wo_s[pl.ds(c * kc, kc), sl], preferred_element_type=F32
+            )
+            return carry
+
+        lax.fori_loop(0, n_count, n_step, 0, unroll=True)
+
+    for k in range(dp_count):
+        stg[pl.ds(k * tokens, tokens), pl.ds(0, tp_count * cols)] = acc_s[
+            pl.ds(k * rows_pad, tokens), :
+        ]
+
+    lane = lax.broadcasted_iota(jnp.int32, (all_tokens, pad), 1)
+    for j in range(tp_count):
+        piece = jnp.where(lane < cols, stg[:, pl.ds(j * cols, pad)], 0.0)
+        red_send[j] = piece.astype(BF16)
+        own_s[j] = piece
+
+    def rs_copy(o):
+        peer = lax.rem(t + o, tp_count)
+        return pltpu.make_async_remote_copy(
+            src_ref=red_send.at[peer],
+            dst_ref=red_recv.at[t],
+            send_sem=rs_send.at[o],
+            recv_sem=rs_recv.at[t],
+            device_id=(g, d, peer),
+            device_id_type=MESH,
+        )
+
+    def rs_arrival(o):
+        src = lax.rem(t + o, tp_count)
+        return pltpu.make_async_remote_copy(
+            src_ref=red_send.at[src],
+            dst_ref=red_recv.at[src],
+            send_sem=rs_send.at[o],
+            recv_sem=rs_recv.at[src],
+            device_id=(g, d, src),
+            device_id_type=MESH,
+        )
+
+    for o in range(1, tp_count):
+        rs_copy(o).start()
+    total = own_s[t] + res_ref[t].astype(F32)
+    for o in range(1, tp_count):
+        rs_arrival(o).wait_recv()
+        total = total + red_recv[lax.rem(t + o, tp_count)].astype(F32)
+    stream = total.astype(BF16)
+    attn_ref[...] = stream[:, :cols]
+
+    packed = jnp.zeros((16 * dp_count, 128), F32)
+    for q in range(4):
+        packed = packed + jnp.dot(
+            onehot_s[q], stream[:, q * 128 : (q + 1) * 128], preferred_element_type=F32
+        )
+    packed = packed.astype(BF16)
+    for p in range(dp_count):
+        disp[p] = packed[p * 16 : (p + 1) * 16]
+
+    def dx_copy(o):
+        other = lax.rem(me + o, peers)
+        return pltpu.make_async_remote_copy(
+            src_ref=disp.at[other // tp_count],
+            dst_ref=xrecv.at[me],
+            send_sem=dx_send.at[o],
+            recv_sem=dx_recv.at[me],
+            device_id=(g, other // tp_count, lax.rem(other, tp_count)),
+            device_id_type=MESH,
+        )
+
+    def dx_arrival(o):
+        src = lax.rem(me + o, peers)
+        return pltpu.make_async_remote_copy(
+            src_ref=disp.at[0],
+            dst_ref=xrecv.at[src],
+            send_sem=dx_send.at[o],
+            recv_sem=dx_recv.at[src],
+            device_id=(g, src // tp_count, lax.rem(src, tp_count)),
+            device_id_type=MESH,
+        )
+
+    for o in range(1, peers):
+        dx_copy(o).start()
+    xrecv[me] = disp[d]
+    wg_copy.wait()
+    wu_copy.wait()
+
+    group = lax.broadcasted_iota(jnp.int32, (16, 128), 0) >> 2
+    acc_g = jnp.zeros((16, ff), F32)
+    acc_u = jnp.zeros((16, ff), F32)
+    squares = jnp.zeros((16, 128), F32)
+
+    def expert_piece(src, carry):
+        acc_g, acc_u, squares = carry
+        values = xrecv[src].astype(F32)
+        scaled = values * gain_ref[src].astype(F32)
+        left = jnp.concatenate(
+            [jnp.where(group == q, scaled, 0.0) for q in range(4)], axis=1
+        ).astype(BF16)
+        sl = pl.ds(pl.multiple_of(src * cols, 64), pad)
+        acc_g = acc_g + jnp.dot(left, wg_s[sl, :], preferred_element_type=F32)
+        acc_u = acc_u + jnp.dot(left, wu_s[sl, :], preferred_element_type=F32)
+        return acc_g, acc_u, squares + values * values
+
+    carry = expert_piece(me, (acc_g, acc_u, squares))
+
+    def expert_step(o, carry):
+        dx_arrival(o).wait_recv()
+        return expert_piece(lax.rem(me + o, peers), carry)
+
+    acc_g, acc_u, squares = lax.fori_loop(1, peers, expert_step, carry)
+
+    def fold(a):
+        return a[0:4] + a[4:8] + a[8:12] + a[12:16]
+
+    mean_square = fold(jnp.sum(squares, axis=1, keepdims=True)) / model
+    scale = lax.rsqrt(mean_square + 1e-06)
+    gate_proj = fold(acc_g) * scale
+    up_proj = fold(acc_u) * scale
+    hidden = sg_s[0:4, 0:1] * (gate_proj / (1.0 + jnp.exp(-gate_proj))) * up_proj
+    hid_ref[0] = hidden[0:capacity].astype(BF16)
+
+    for c in range(chunks):
+        for o in range(1, dp_count):
+            ag_copy(c, o).wait_send()
+    for o in range(1, tp_count):
+        rs_copy(o).wait_send()
+    for o in range(1, peers):
+        dx_copy(o).wait_send()
+
+
+UNROLL = 2
+
+
+def fused_layer(
+    queries,
+    latent_cache,
+    lengths,
+    value_up,
+    out_proj,
+    residual,
+    expert_ids,
+    gate_weights,
+    placement,
+    norm_gain,
+    w_gate,
+    w_up,
+):
+    dp_count = lax.axis_size("dp")
+    tp_count = lax.axis_size("tensor")
+    all_tokens = expert_ids.shape[0]
+    capacity = max(2, all_tokens * TOPK * 2 // EXPERTS)
+    tokens, heads, width = queries.shape
+    cols = residual.shape[1] // tp_count
+    model = norm_gain.shape[0]
+    ff = w_gate.shape[2]
+    pad = 512
+    chunks = 4
+    rows_pad = 16
+    peers = dp_count * tp_count
+    hpc = heads // chunks
+    gain = jnp.pad(norm_gain.reshape(peers, cols), ((0, 0), (0, pad - cols)))
+    gain = jnp.broadcast_to(gain.reshape(peers, 4, 1, 128), (peers, 4, 4, 128)).reshape(
+        peers, 16, 128
+    )
+    res = jnp.pad(
+        residual.reshape(all_tokens, tp_count, cols).transpose(1, 0, 2),
+        ((0, 0), (0, 0), (0, pad - cols)),
+    )
+    hbm = pl.BlockSpec(memory_space=pl.ANY)
+    vmem = pl.BlockSpec(memory_space=pltpu.VMEM)
+    smem = pl.BlockSpec(memory_space=pltpu.SMEM)
+    dma = pltpu.SemaphoreType.DMA
+    return pl.pallas_call(
+        functools.partial(layer_kernel, dp_count, tp_count),
+        out_shape=(
+            jax.ShapeDtypeStruct((all_tokens, cols), BF16),
+            jax.ShapeDtypeStruct((1, capacity, ff), BF16),
+        ),
+        in_specs=[hbm, hbm, smem, hbm, hbm, vmem, vmem, vmem, vmem, vmem, hbm, hbm],
+        out_specs=(vmem, vmem),
+        scratch_shapes=[
+            pltpu.VMEM((tokens, heads, width), BF16),
+            pltpu.VMEM((tokens, width, latent_cache.shape[1]), BF16),
+            pltpu.VMEM(value_up.shape, BF16),
+            pltpu.VMEM(out_proj.shape, BF16),
+            pltpu.VMEM((model + pad - cols, ff), BF16),
+            pltpu.VMEM((model + pad - cols, ff), BF16),
+            pltpu.VMEM((LATENT // 128, heads * rows_pad, 128), F32),
+            pltpu.VMEM((chunks, dp_count, rows_pad, hpc * VHEAD), BF16),
+            pltpu.VMEM((dp_count * rows_pad, tp_count * cols), F32),
+            pltpu.VMEM((all_tokens, tp_count * cols + 128), F32),
+            pltpu.VMEM((tp_count, all_tokens, pad), F32),
+            pltpu.VMEM((tp_count, all_tokens, pad), BF16),
+            pltpu.VMEM((tp_count, all_tokens, pad), BF16),
+            pltpu.VMEM((4, 16 * dp_count, all_tokens), BF16),
+            pltpu.VMEM((dp_count, 16, 128), BF16),
+            pltpu.VMEM((peers, 16, 128), BF16),
+            pltpu.VMEM((8, 128), F32),
+            dma((2,)),
+            dma((chunks,)),
+            dma((chunks,)),
+            dma((2,)),
+            dma((chunks, dp_count)),
+            dma((chunks, dp_count)),
+            dma((tp_count,)),
+            dma((tp_count,)),
+            dma((peers,)),
+            dma((peers,)),
+        ],
+        compiler_params=pltpu.CompilerParams(
+            collective_id=0, has_side_effects=True, vmem_limit_bytes=58 * 1024 * 1024
+        ),
+    )(
+        queries,
+        jnp.swapaxes(latent_cache, 1, 2),
+        lengths,
+        value_up,
+        out_proj,
+        res,
+        expert_ids.T,
+        gate_weights.T,
+        placement.reshape(1, -1),
+        gain,
+        w_gate,
+        w_up,
+    )
 
 
 def slot_table(expert_ids, placement, held_count, capacity):
@@ -119,6 +577,24 @@
         P("dp", None, "tensor"),
     )
     out_specs = (P("groups", ("dp", "tensor")), P(("groups", "dp"), None, "tensor"))
+
+    def layer(*args):
+        token_count = args[6].shape[0]
+        capacity = max(2, token_count * TOPK * 2 // EXPERTS)
+        cols = args[5].shape[1] // mesh.shape["tensor"]
+        fits = (
+            args[10].shape[0] == 1
+            and capacity <= 4
+            and 384 < cols <= 512
+            and cols % 64 == 0
+            and args[5].shape[1] % 256 == 0
+            and args[0].shape[0] <= 16
+            and args[0].shape[1] % 4 == 0
+            and mesh.shape["dp"] < 8
+            and token_count % 16 == 0
+        )
+        return (fused_layer if fits else on_device)(*args)
+
     return jax.shard_map(
-        on_device, mesh=mesh, in_specs=in_specs, out_specs=out_specs, check_vma=False
-    )
+        layer, mesh=mesh, in_specs=in_specs, out_specs=out_specs, check_vma=False
+    )

time: 104 us -> 42.1 us (0.40)
  waiting for transfers between devices: 36.4 us -> 0 us
  Pallas kernels: 0 us -> 35.1 us
  matrix products: 24.5 us -> 0 us
  blocking collectives: 17.4 us -> 0 us
  between operations: 14.2 us -> 0.66 us
  starting transfers between devices: 4.64 us -> 0 us
  other arithmetic: 4.23 us -> 0 us
  local copies, waits for them, and re-layouts: 2.47 us -> 6.04 us
    pallas_call x0 -> x1, Pallas kernels: none -> 35.1 us  [fused_layer(): pl.pallas_call(functools.partial(layer_kernel, dp_count, tp_count), out_s...]
    psum x1 -> x0, waiting for transfers between devices: 31.4 us -> none  [on_device(): summed_all = lax.psum(partial_sum, 'tensor')]
    dot_general x7 -> x0, matrix products: 24.5 us -> none  [the longest x1 8.53 us: on_device(): jnp.dot(lax.all_gather(head_out, 'dp', axis=0, tiled=True), out_proj, pre...]
    all_gather x1 -> x0, blocking collectives: 17.4 us -> none  [on_device(): lax.all_gather(head_out, 'dp', axis=0, tiled=True)]
    all_to_all x1 -> x0, waiting for transfers between devices: 5.02 us -> none  [on_device(): lax.all_to_all(buffer, 'dp', split_axis=0, concat_axis=2, tiled=True)]
    all_to_all x1 -> x0, starting transfers between devices: 4.6 us -> none  [on_device(): lax.all_to_all(buffer, 'dp', split_axis=0, concat_axis=2, tiled=True)]
    unnamed x15 -> x2, local copies, waits for them, and re-layouts: 0.51 us -> 2.7 us
    another operation x2 -> x0, other arithmetic: 1.41 us -> none
  transfers between devices with their start and end apart: 2 -> 0, of which waited for: 2 -> 0; matrix products, arithmetic and copies ran while one was open for 3% -> 0% of each run, Pallas kernels for 0% -> 0%
where the time goes in v1:
time: 42.1 us; the launch traced here: 41.8 us
  Pallas kernels  35.1 us (83%)
  local copies, waits for them, and re-layouts  6.04 us (14%)
  between operations  0.66 us (2%)
    pallas_call x1, Pallas kernels, fused_layer(): pl.pallas_call(functools.partial(layer_kernel, dp_count, tp_count), out_s...  35.1 us
    unnamed x2, local copies, waits for them, and re-layouts  2.7 us
    reshape x2, local copies, waits for them, and re-layouts, fused_layer(): residual.reshape(all_tokens, tp_count, cols).transpose(1, 0, 2)  1.18 us

profile of v1, /device:TPU:0, one launch (start us, length us, event | category | flops | bytes accessed | tf_op | source)
XLA Modules:
  0.0 41.8 jit_solution(6556001870509508163)
XLA Ops:
  0.6 1.1 %reshape.18 = bf16[48,4,448]{2,1,0:T(4,128)(2,1)S(1)} reshape(bf16[48,1792]{1,0:T(8,128)(2,1)} %param.17) | data formatting | bytes 344064 | tf_op jit(solution)/shard_map/reshape | solution.py:408
  1.8 0.7 %pad.8.res_ref = bf16[4,48,512]{2,1,0:T(8,128)(2,1)} pad(bf16[4,48,448]{2,1,0:T(8,128)(2,1)S(1)} %bitcast.9, bf16[]{:T(256)} %constant.2.clone.1), padding=0_0x0_0x0_64 | pad | bytes 368642 | tf_op jit(solution)/shard_map/jit(_pad)/pad | solution.py:407
  2.5 0.8 %reshape.20 = bf16[16,448]{1,0:T(8,128)(2,1)S(1)} reshape(bf16[7168]{0:T(1024)(128)(2,1)} %param.21) | data formatting | bytes 28672 | tf_op jit(solution)/shard_map/reshape | solution.py:403
  3.3 0.7 %broadcast_in_dim.8 = bf16[16,4,4,128]{3,2,1,0:T(4,128)(2,1)} broadcast(bf16[16,4,128]{2,1,0:T(4,128)(2,1)S(1)} %broadcast_in_dim.7), dimensions={0,1,3} | broadcast | bytes 81920 | tf_op jit(solution)/shard_map/broadcast_in_dim | solution.py:404
  4.0 35.1 %shard_map.131 = (bf16[48,448]{1,0:T(8,128)(2,1)}, bf16[1,3,512]{2,1,0:T(4,128)(2,1)}) custom-call(bf16[12,32,576]{2,1,0:T(8,128)(2,1)} %q_hbm.1, bf16[12,576,128]{2,1,0:T(8,128)(2,1)} %bitcast.8, s32[12]{0:T(128)} %len_ref.1, bf16[32,512,128]{2,1,0:T(8,128)(2,1)} %vu_hbm.1, bf16[4096,1792]{1,0:T(8,128)(2,1)} %wo_hbm.1, bf16[4,48,512]{2,1,0:T(8,128)(2,1)} %pad.8.res_ref, ...), custom_call_target="tpu_custom_call" | custom-call | tf_op jit(solution)/shard_map/pallas_call | solution.py:415
  39.1 1.4 %copy.19 = bf16[48,448]{1,0:T(8,128)(2,1)} copy(bf16[48,448]{1,0:T(8,128)(2,1)} %get-tuple-element.4) | data formatting | bytes 86016
  40.5 1.3 %copy.20 = bf16[1,3,512]{2,1,0:T(4,128)(2,1)} copy(bf16[1,3,512]{2,1,0:T(4,128)(2,1)} %get-tuple-element.5) | data formatting | bytes 6144
  (3 shorter events, 0.1 us)

commit v2 on v1

--- a/solution.py
+++ b/solution.py
@@ -42,7 +42,10 @@
     wu_s,
     ctx_s,
     hbuf,
-    acc_s,
+    pack_s,
+    lhs_s,
+    gain_a,
+    gain_s,
     stg,
     own_s,
     red_send,
@@ -160,9 +163,29 @@
     ctx_s[...] = jnp.zeros_like(ctx_s)
     wg_s[pl.ds(model, wg_s.shape[0] - model), :] = jnp.zeros((wg_s.shape[0] - model, ff), BF16)
     wu_s[pl.ds(model, wu_s.shape[0] - model), :] = jnp.zeros((wu_s.shape[0] - model, ff), BF16)
-    stg[:, pl.ds(tp_count * cols, stg.shape[1] - tp_count * cols)] = jnp.zeros(
-        (all_tokens, stg.shape[1] - tp_count * cols), F32
-    )
+    total_cols = tp_count * cols
+    stg[:, pl.ds(total_cols, stg.shape[1] - total_cols)] = jnp.zeros(
+        (all_tokens, stg.shape[1] - total_cols), F32
+    )
+    stg[:, pl.ds(0, total_cols)] = res_ref[...].astype(F32)
+    lane = lax.broadcasted_iota(jnp.int32, (all_tokens, pad), 1)
+    for j in range(tp_count):
+        own_s[j] = jnp.where(lane < cols, stg[:, pl.ds(j * cols, pad)], 0.0)
+
+    gain_rows = gain_ref.shape[0]
+    gain_a[pl.ds(0, gain_rows), :] = gain_ref[...].astype(F32)
+    gain_a[pl.ds(gain_rows, 8), :] = jnp.zeros((8, 128), F32)
+    half = lax.broadcasted_iota(jnp.int32, (1, 128), 1) >= 64
+    group = lax.broadcasted_iota(jnp.int32, (16, 128), 0) >> 2
+    for src in range(peers):
+        first, odd = divmod(src * cols, 128)
+        block = jnp.zeros((16, 128), F32)
+        for q in range(4):
+            row = gain_a[pl.ds(first + q, 1), :]
+            if odd:
+                row = pltpu.roll(jnp.where(half, row, gain_a[pl.ds(first + q + 1, 1), :]), 64, 1)
+            block = jnp.where(group == q, row, block)
+        gain_s[src] = block
 
     q_copy.wait()
     c_copy.wait()
@@ -193,27 +216,46 @@
 
     lax.fori_loop(0, tokens, token_step, 0, unroll=UNROLL)
 
-    def ag_copy(c, o):
-        peer = lax.rem(d + o, dp_count)
+    def ag_copy(c, origin, right):
         return pltpu.make_async_remote_copy(
-            src_ref=hbuf.at[c, d],
-            dst_ref=hbuf.at[c, d],
-            send_sem=ag_send.at[c, o],
-            recv_sem=ag_recv.at[c, d],
-            device_id=(g, peer, t),
+            src_ref=hbuf.at[c, origin],
+            dst_ref=hbuf.at[c, origin],
+            send_sem=ag_send.at[c, origin, 0 if right else 1],
+            recv_sem=ag_recv.at[c, origin],
+            device_id=(g, d + 1 if right else d - 1, t),
             device_id_type=MESH,
         )
 
-    def ag_arrival(c, o):
-        src = lax.rem(d + o, dp_count)
-        return pltpu.make_async_remote_copy(
-            src_ref=hbuf.at[c, src],
-            dst_ref=hbuf.at[c, src],
-            send_sem=ag_send.at[c, o],
-            recv_sem=ag_recv.at[c, src],
-            device_id=(g, src, t),
-            device_id_type=MESH,
-        )
+    def ag_each(c, stage, act):
+        @pl.when((d >= stage) & (d < dp_count - 1))
+        def _():
+            act(ag_copy(c, d - stage, True), stage)
+
+        @pl.when((d + stage < dp_count) & (d > 0))
+        def _():
+            act(ag_copy(c, d + stage, False), stage)
+
+    def pass_on(copy, stage):
+        if stage:
+            copy.wait_recv()
+        copy.start()
+
+    def last_arrival(c):
+        @pl.when(d == dp_count - 1)
+        def _():
+            for o in range(dp_count - 1):
+                ag_copy(c, o, False).wait_recv()
+
+        @pl.when(d == 0)
+        def _():
+            for o in range(1, dp_count):
+                ag_copy(c, o, True).wait_recv()
+
+    def forward(step):
+        for stage in range(1, dp_count - 1):
+            c = step - stage
+            if 0 <= c < chunks:
+                ag_each(c, stage, pass_on)
 
     for c in range(chunks):
         vu_copies[c].wait()
@@ -223,40 +265,35 @@
                 [ctx_s[k, pl.ds(h * rows_pad, rows_pad), :] for k in range(LATENT // 128)], axis=1
             ).astype(BF16)
             out = jnp.dot(rows, vu_s[h], preferred_element_type=F32)
-            hbuf[c, d, :, pl.ds(hl * VHEAD, VHEAD)] = out.astype(BF16)
+            pack_s[pl.ds(hl * tokens, tokens), :] = out[:tokens]
+        hbuf[c, d] = pack_s[...].astype(BF16)
         if c == 0:
             pl.semaphore_wait(barrier, peers - 1)
-        for o in range(1, dp_count):
-            ag_copy(c, o).start()
-
-    acc_s[...] = jnp.zeros_like(acc_s)
+        ag_each(c, 0, pass_on)
+        forward(c)
+
     n_tile = 256
     n_count = wo_s.shape[1] // n_tile
     for c in range(chunks):
+        forward(chunks + c)
         wo_copies[c].wait()
-        for o in range(1, dp_count):
-            ag_arrival(c, o).wait_recv()
-        left = hbuf[c].reshape(dp_count * rows_pad, kc)
-
-        def n_step(n, carry, c=c, left=left):
-            sl = pl.ds(pl.multiple_of(n * n_tile, n_tile), n_tile)
-            acc_s[:, sl] += jnp.dot(
-                left, wo_s[pl.ds(c * kc, kc), sl], preferred_element_type=F32
-            )
-            return carry
-
-        lax.fori_loop(0, n_count, n_step, 0, unroll=True)
-
-    for k in range(dp_count):
-        stg[pl.ds(k * tokens, tokens), pl.ds(0, tp_count * cols)] = acc_s[
-            pl.ds(k * rows_pad, tokens), :
-        ]
-
-    lane = lax.broadcasted_iota(jnp.int32, (all_tokens, pad), 1)
+        last_arrival(c)
+        for src in range(dp_count):
+            block = hbuf[c, src].astype(F32)
+            for hl in range(hpc):
+                lhs_s[pl.ds(src * tokens, tokens), pl.ds(hl * VHEAD, VHEAD)] = block[
+                    hl * tokens : (hl + 1) * tokens
+                ]
+        left = lhs_s[...].astype(BF16)
+        for n in range(n_count):
+            sl = pl.ds(n * n_tile, n_tile)
+            out = jnp.dot(left, wo_s[pl.ds(c * kc, kc), sl], preferred_element_type=F32)
+            stg[:, sl] = out if c == 0 else stg[:, sl] + out
+
     for j in range(tp_count):
         piece = jnp.where(lane < cols, stg[:, pl.ds(j * cols, pad)], 0.0)
         red_send[j] = piece.astype(BF16)
-        own_s[j] = piece
+        own_s[j] = own_s[j] + piece
 
     def rs_copy(o):
         peer = lax.rem(t + o, tp_count)
@@ -282,7 +319,7 @@
 
     for o in range(1, tp_count):
         rs_copy(o).start()
-    total = own_s[t] + res_ref[t].astype(F32)
+    total = own_s[t]
     for o in range(1, tp_count):
         rs_arrival(o).wait_recv()
         total = total + red_recv[lax.rem(t + o, tp_count)].astype(F32)
@@ -326,7 +363,6 @@
     wg_copy.wait()
     wu_copy.wait()
 
-    group = lax.broadcasted_iota(jnp.int32, (16, 128), 0) >> 2
     acc_g = jnp.zeros((16, ff), F32)
     acc_u = jnp.zeros((16, ff), F32)
     squares = jnp.zeros((16, 128), F32)
@@ -334,7 +370,7 @@
     def expert_piece(src, carry):
         acc_g, acc_u, squares = carry
         values = xrecv[src].astype(F32)
-        scaled = values * gain_ref[src].astype(F32)
+        scaled = values * gain_s[src]
         left = jnp.concatenate(
             [jnp.where(group == q, scaled, 0.0) for q in range(4)], axis=1
         ).astype(BF16)
@@ -362,15 +398,15 @@
     hid_ref[0] = hidden[0:capacity].astype(BF16)
 
     for c in range(chunks):
-        for o in range(1, dp_count):
-            ag_copy(c, o).wait_send()
+        for stage in range(dp_count - 1):
+            ag_each(c, stage, lambda copy, stage: copy.wait_send())
     for o in range(1, tp_count):
         rs_copy(o).wait_send()
     for o in range(1, peers):
         dx_copy(o).wait_send()
 
 
-UNROLL = 2
+UNROLL = 4
 
 
 def fused_layer(
@@ -400,14 +436,6 @@
     rows_pad = 16
     peers = dp_count * tp_count
     hpc = heads // chunks
-    gain = jnp.pad(norm_gain.reshape(peers, cols), ((0, 0), (0, pad - cols)))
-    gain = jnp.broadcast_to(gain.reshape(peers, 4, 1, 128), (peers, 4, 4, 128)).reshape(
-        peers, 16, 128
-    )
-    res = jnp.pad(
-        residual.reshape(all_tokens, tp_count, cols).transpose(1, 0, 2),
-        ((0, 0), (0, 0), (0, pad - cols)),
-    )
     hbm = pl.BlockSpec(memory_space=pl.ANY)
     vmem = pl.BlockSpec(memory_space=pltpu.VMEM)
     smem = pl.BlockSpec(memory_space=pltpu.SMEM)
@@ -428,8 +456,11 @@
             pltpu.VMEM((model + pad - cols, ff), BF16),
             pltpu.VMEM((model + pad - cols, ff), BF16),
             pltpu.VMEM((LATENT // 128, heads * rows_pad, 128), F32),
-            pltpu.VMEM((chunks, dp_count, rows_pad, hpc * VHEAD), BF16),
-            pltpu.VMEM((dp_count * rows_pad, tp_count * cols), F32),
+            pltpu.VMEM((chunks, dp_count, hpc * tokens, VHEAD), BF16),
+            pltpu.VMEM((hpc * tokens, VHEAD), F32),
+            pltpu.VMEM((dp_count * tokens, hpc * VHEAD), F32),
+            pltpu.VMEM((model // 128 + 8, 128), F32),
+            pltpu.VMEM((peers, 16, 128), F32),
             pltpu.VMEM((all_tokens, tp_count * cols + 128), F32),
             pltpu.VMEM((tp_count, all_tokens, pad), F32),
             pltpu.VMEM((tp_count, all_tokens, pad), BF16),
@@ -442,7 +473,7 @@
             dma((chunks,)),
             dma((chunks,)),
             dma((2,)),
-            dma((chunks, dp_count)),
+            dma((chunks, dp_count, 2)),
             dma((chunks, dp_count)),
             dma((tp_count,)),
             dma((tp_count,)),
@@ -458,11 +489,11 @@
         lengths,
         value_up,
         out_proj,
-        res,
+        residual,
         expert_ids.T,
         gate_weights.T,
         placement.reshape(1, -1),
-        gain,
+        norm_gain.reshape(-1, 128),
         w_gate,
         w_up,
     )
@@ -592,6 +623,7 @@
             and args[0].shape[1] % 4 == 0
             and mesh.shape["dp"] < 8
             and token_count % 16 == 0
+            and args[0].shape[1] // 4 * args[0].shape[0] % 16 == 0
         )
         return (fused_layer if fits else on_device)(*args)
 

time: 42.1 us -> 40.4 us (0.960)
  local copies, waits for them, and re-layouts: 6.04 us -> 2.69 us
  Pallas kernels: 35.1 us -> 36.8 us
    reshape x3 -> x0, local copies, waits for them, and re-layouts: 1.98 us -> none  [the longest x2 1.18 us: fused_layer(): residual.reshape(all_tokens, tp_count, cols).transpose(1, 0, 2)]
    pallas_call x1, Pallas kernels: 35.1 us -> 36.8 us  [fused_layer(): pl.pallas_call(functools.partial(layer_kernel, dp_count, tp_count), out_s...]
    pad x2 -> x0, local copies, waits for them, and re-layouts: 0.7 us -> none  [the longest x1 0.7 us: fused_layer(): jnp.pad(residual.reshape(all_tokens, tp_count, cols).transpose(1, 0, 2),...]
    broadcast_in_dim x2 -> x0, local copies, waits for them, and re-layouts: 0.67 us -> none  [fused_layer(): jnp.broadcast_to(gain.reshape(peers, 4, 1, 128), (peers, 4, 4, 128))]
where the time goes in v2:
time: 40.4 us; the launch traced here: 40.2 us
  Pallas kernels  36.8 us (91%)
  local copies, waits for them, and re-layouts  2.69 us (7%)
  between operations  0.64 us (2%)
    pallas_call x1, Pallas kernels, fused_layer(): pl.pallas_call(functools.partial(layer_kernel, dp_count, tp_count), out_s...  36.8 us
    unnamed x2, local copies, waits for them, and re-layouts  2.69 us

profile of v2, /device:TPU:0, one launch (start us, length us, event | category | flops | bytes accessed | tf_op | source)
XLA Modules:
  0.0 40.2 jit_solution(13465682398033782681)
XLA Ops:
  0.6 36.8 %shard_map.131 = (bf16[48,448]{1,0:T(8,128)(2,1)}, bf16[1,3,512]{2,1,0:T(4,128)(2,1)}) custom-call(bf16[12,32,576]{2,1,0:T(8,128)(2,1)} %q_hbm.1, bf16[12,576,128]{2,1,0:T(8,128)(2,1)} %bitcast.5, s32[12]{0:T(128)} %len_ref.1, bf16[32,512,128]{2,1,0:T(8,128)(2,1)} %vu_hbm.1, bf16[4096,1792]{1,0:T(8,128)(2,1)} %wo_hbm.1, bf16[48,1792]{1,0:T(8,128)(2,1)} %res_ref.1, ...), custom_call_target="tpu_custom_call" | custom-call | tf_op jit(solution)/shard_map/pallas_call | solution.py:443
  37.5 1.4 %copy.16 = bf16[48,448]{1,0:T(8,128)(2,1)} copy(bf16[48,448]{1,0:T(8,128)(2,1)} %get-tuple-element.4) | data formatting | bytes 86016
  38.9 1.3 %copy.17 = bf16[1,3,512]{2,1,0:T(4,128)(2,1)} copy(bf16[1,3,512]{2,1,0:T(4,128)(2,1)} %get-tuple-element.5) | data formatting | bytes 6144

commit v3 on v2

--- a/solution.py
+++ b/solution.py
@@ -111,9 +111,6 @@
     ]
     wg_copy = pltpu.make_async_copy(wg_hbm.at[0], wg_s.at[pl.ds(0, model)], we_sem.at[0])
     wu_copy = pltpu.make_async_copy(wu_hbm.at[0], wu_s.at[pl.ds(0, model)], we_sem.at[1])
-    for cp in vu_copies:
-        cp.start()
-
     ids = ids_ref[...]
     gates = gates_ref[...]
     place = place_ref[...]
@@ -189,6 +186,8 @@
 
     q_copy.wait()
     c_copy.wait()
+    for cp in vu_copies:
+        cp.start()
     for cp in wo_copies:
         cp.start()
     wg_copy.start()
@@ -216,46 +215,39 @@
 
     lax.fori_loop(0, tokens, token_step, 0, unroll=UNROLL)
 
-    def ag_copy(c, origin, right):
+    def ag_copy(c, stage, right):
         return pltpu.make_async_remote_copy(
-            src_ref=hbuf.at[c, origin],
-            dst_ref=hbuf.at[c, origin],
-            send_sem=ag_send.at[c, origin, 0 if right else 1],
-            recv_sem=ag_recv.at[c, origin],
-            device_id=(g, d + 1 if right else d - 1, t),
+            src_ref=hbuf.at[c, d],
+            dst_ref=hbuf.at[c, d],
+            send_sem=ag_send.at[c, stage, 0 if right else 1],
+            recv_sem=ag_recv.at[c, d],
+            device_id=(g, d + stage + 1 if right else d - stage - 1, t),
             device_id_type=MESH,
         )
 
     def ag_each(c, stage, act):
-        @pl.when((d >= stage) & (d < dp_count - 1))
+        @pl.when(d + stage + 1 < dp_count)
         def _():
-            act(ag_copy(c, d - stage, True), stage)
-
-        @pl.when((d + stage < dp_count) & (d > 0))
+            act(ag_copy(c, stage, True), stage)
+
+        @pl.when(d - stage - 1 >= 0)
         def _():
-            act(ag_copy(c, d + stage, False), stage)
-
-    def pass_on(copy, stage):
-        if stage:
-            copy.wait_recv()
+            act(ag_copy(c, stage, False), stage)
+
+    def launch(copy, stage):
         copy.start()
 
     def last_arrival(c):
-        @pl.when(d == dp_count - 1)
-        def _():
-            for o in range(dp_count - 1):
-                ag_copy(c, o, False).wait_recv()
-
-        @pl.when(d == 0)
-        def _():
-            for o in range(1, dp_count):
-                ag_copy(c, o, True).wait_recv()
-
-    def forward(step):
-        for stage in range(1, dp_count - 1):
-            c = step - stage
-            if 0 <= c < chunks:
-                ag_each(c, stage, pass_on)
+        for o in range(1, dp_count):
+            src = lax.rem(d + o, dp_count)
+            pltpu.make_async_remote_copy(
+                src_ref=hbuf.at[c, src],
+                dst_ref=hbuf.at[c, src],
+                send_sem=ag_send.at[c, 0, 0],
+                recv_sem=ag_recv.at[c, src],
+                device_id=(g, src, t),
+                device_id_type=MESH,
+            ).wait_recv()
 
     for c in range(chunks):
         vu_copies[c].wait()
@@ -269,13 +261,12 @@
         hbuf[c, d] = pack_s[...].astype(BF16)
         if c == 0:
             pl.semaphore_wait(barrier, peers - 1)
-        ag_each(c, 0, pass_on)
-        forward(c)
+        for stage in reversed(range(dp_count - 1)):
+            ag_each(c, stage, launch)
 
     n_tile = 256
     n_count = wo_s.shape[1] // n_tile
     for c in range(chunks):
-        forward(chunks + c)
         wo_copies[c].wait()
         last_arrival(c)
         for src in range(dp_count):
@@ -385,7 +376,7 @@
         dx_arrival(o).wait_recv()
         return expert_piece(lax.rem(me + o, peers), carry)
 
-    acc_g, acc_u, squares = lax.fori_loop(1, peers, expert_step, carry)
+    acc_g, acc_u, squares = lax.fori_loop(1, peers, expert_step, carry, unroll=True)
 
     def fold(a):
         return a[0:4] + a[4:8] + a[8:12] + a[12:16]
@@ -443,8 +434,8 @@
     return pl.pallas_call(
         functools.partial(layer_kernel, dp_count, tp_count),
         out_shape=(
-            jax.ShapeDtypeStruct((all_tokens, cols), BF16),
-            jax.ShapeDtypeStruct((1, capacity, ff), BF16),
+            pltpu.VMEM((all_tokens, cols), BF16),
+            pltpu.VMEM((1, capacity, ff), BF16),
         ),
         in_specs=[hbm, hbm, smem, hbm, hbm, vmem, vmem, vmem, vmem, vmem, hbm, hbm],
         out_specs=(vmem, vmem),

time: 40.4 us -> 34.6 us (0.86)
  Pallas kernels: 36.8 us -> 32.4 us
  local copies, waits for them, and re-layouts: 2.69 us -> 1.21 us
    pallas_call x1, Pallas kernels: 36.8 us -> 32.4 us  [fused_layer(): pl.pallas_call(functools.partial(layer_kernel, dp_count, tp_count), out_s...]
    unnamed x2, local copies, waits for them, and re-layouts: 2.69 us -> 1.21 us
where the time goes in v3:
time: 34.6 us; the launch traced here: 34.3 us
  Pallas kernels  32.4 us (94%)
  local copies, waits for them, and re-layouts  1.21 us (3%)
  between operations  0.64 us (2%)
    pallas_call x1, Pallas kernels, fused_layer(): pl.pallas_call(functools.partial(layer_kernel, dp_count, tp_count), out_s...  32.4 us
    unnamed x2, local copies, waits for them, and re-layouts  1.21 us

profile of v3, /device:TPU:0, one launch (start us, length us, event | category | flops | bytes accessed | tf_op | source)
XLA Modules:
  0.0 34.3 jit_solution(12960806797495437569)
XLA Ops:
  0.6 32.4 %shard_map.131 = (bf16[48,448]{1,0:T(8,128)(2,1)S(1)}, bf16[1,3,512]{2,1,0:T(4,128)(2,1)S(1)}) custom-call(bf16[12,32,576]{2,1,0:T(8,128)(2,1)} %q_hbm.1, bf16[12,576,128]{2,1,0:T(8,128)(2,1)} %bitcast.5, s32[12]{0:T(128)} %len_ref.1, bf16[32,512,128]{2,1,0:T(8,128)(2,1)} %vu_hbm.1, bf16[4096,1792]{1,0:T(8,128)(2,1)} %wo_hbm.1, bf16[48,1792]{1,0:T(8,128)(2,1)} %res_ref.1, ...), custom_call_target="tpu_custom_call" | custom-call | tf_op jit(solution)/shard_map/pallas_call | solution.py:434
  33.1 0.6 %copy.16 = bf16[48,448]{1,0:T(8,128)(2,1)} copy(bf16[48,448]{1,0:T(8,128)(2,1)S(1)} %get-tuple-element.2) | data formatting | bytes 86016
  33.7 0.6 %copy.17 = bf16[1,3,512]{2,1,0:T(4,128)(2,1)} copy(bf16[1,3,512]{2,1,0:T(4,128)(2,1)S(1)} %get-tuple-element.3) | data formatting | bytes 6144

commit v4 on v3

--- a/solution.py
+++ b/solution.py
@@ -423,7 +423,7 @@
     model = norm_gain.shape[0]
     ff = w_gate.shape[2]
     pad = 512
-    chunks = 4
+    chunks = 8
     rows_pad = 16
     peers = dp_count * tp_count
     hpc = heads // chunks
@@ -611,10 +611,10 @@
             and cols % 64 == 0
             and args[5].shape[1] % 256 == 0
             and args[0].shape[0] <= 16
-            and args[0].shape[1] % 4 == 0
+            and args[0].shape[1] % 8 == 0
             and mesh.shape["dp"] < 8
             and token_count % 16 == 0
-            and args[0].shape[1] // 4 * args[0].shape[0] % 16 == 0
+            and args[0].shape[1] // 8 * args[0].shape[0] % 16 == 0
         )
         return (fused_layer if fits else on_device)(*args)
 

time: 34.6 us -> 34.8 us (level)
  no operation moved by 1% of the time
where the time goes in v4:
time: 34.8 us; the launch traced here: 34.6 us
  Pallas kernels  32.7 us (94%)
  local copies, waits for them, and re-layouts  1.21 us (3%)
  between operations  0.64 us (2%)
    pallas_call x1, Pallas kernels, fused_layer(): pl.pallas_call(functools.partial(layer_kernel, dp_count, tp_count), out_s...  32.7 us
    unnamed x2, local copies, waits for them, and re-layouts  1.21 us

profile of v4, /device:TPU:0, one launch (start us, length us, event | category | flops | bytes accessed | tf_op | source)
XLA Modules:
  0.0 34.6 jit_solution(16150366197618882763)
XLA Ops:
  0.6 32.7 %shard_map.131 = (bf16[48,448]{1,0:T(8,128)(2,1)S(1)}, bf16[1,3,512]{2,1,0:T(4,128)(2,1)S(1)}) custom-call(bf16[12,32,576]{2,1,0:T(8,128)(2,1)} %q_hbm.1, bf16[12,576,128]{2,1,0:T(8,128)(2,1)} %bitcast.5, s32[12]{0:T(128)} %len_ref.1, bf16[32,512,128]{2,1,0:T(8,128)(2,1)} %vu_hbm.1, bf16[4096,1792]{1,0:T(8,128)(2,1)} %wo_hbm.1, bf16[48,1792]{1,0:T(8,128)(2,1)} %res_ref.1, ...), custom_call_target="tpu_custom_call" | custom-call | tf_op jit(solution)/shard_map/pallas_call | solution.py:434
  33.4 0.6 %copy.16 = bf16[48,448]{1,0:T(8,128)(2,1)} copy(bf16[48,448]{1,0:T(8,128)(2,1)S(1)} %get-tuple-element.2) | data formatting | bytes 86016
  34.0 0.6 %copy.17 = bf16[1,3,512]{2,1,0:T(4,128)(2,1)} copy(bf16[1,3,512]{2,1,0:T(4,128)(2,1)S(1)} %get-tuple-element.3) | data formatting | bytes 6144
